TPU v7x, 512 devices: a whole 4x4x16 slice. The times are simulated.
512 devices in a mesh: tm: 16 (over x, y), users: 8 (over z_lo), mp: 4 (over z_hi, core).
Axes of the slice: x: 4, y: 4, z: 16 (z_hi: 2, z_lo: 8; z = z_hi * 8 + z_lo), core: 2. Of those that a mesh axis runs over, the one named last changes fastest.
Arguments:
- history: bfloat16 [32, 4096, 512], P(('users', 'mp'), 'tm'), may hold values from -6 to 6
- ln_gain: float32 [512], replicated, may hold values from 0.1 to 1.9
- w_proj: bfloat16 [512, 2048], replicated, may hold values from -18 to 18
- w_out: bfloat16 [512, 512], replicated, may hold values from -0.25 to 0.25
- pool_query: bfloat16 [4, 512], replicated, may hold values from -0.25 to 0.25
- lengths: int32 [32], P(('users', 'mp')), may hold values from 256 to 4096, as said below
- slots: int32 [32], replicated, may hold values from 0 to 31, each once
- cand_ids: int32 [32, 1024], P('users', 'tm'), may hold values from 0 to 511
- item_table: bfloat16 [4096, 512], P('users'), may hold values from -6 to 6
- w_rank: bfloat16 [1024, 1024], P(None, 'mp'), may hold values from -0.1875 to 0.1875
- b_rank: float32 [1024], P('mp'), may hold values from -1 to 1
- w_score: float32 [1024], P('mp'), may hold values from -0.1875 to 0.1875
Outputs:
- layer_out: bfloat16 [32, 4096, 512], P(('users', 'mp'), 'tm')
- scores: float32 [32, 1024], P('users', 'tm')
Inputs may be any that keep to these rules, and one draw needn't show every extreme that they name: `lengths`: at least one user has history length exactly 4096. `slots`: each user has its own ranker slot; slot s belongs to ranker owner s // 4.
All inputs are finite; a program needn't handle non-finite values.
Results may differ from a plain program's by a relative error of at most 0.015.
Values may be sent and summed in bfloat16 or wider, within the bound.
A program may use at most 128 MiB of HBM per device.

v0:
```python
import jax
import jax.numpy as jnp
from jax import lax
from jax.experimental import pallas as pl
from jax.experimental.pallas import tpu as pltpu
from jax.sharding import PartitionSpec as P

HEADS = 4
SIDE = 4
EPS = 1e-05
VMEM_BYTES = 64 * 1024 * 1024
MESH = pl.DeviceIdType.MESH
STEPS = sorted(
    ((a, b) for a in range(SIDE) for b in range(SIDE) if a or b),
    key=lambda step: -sum(min(n, SIDE - n) for n in step),
)
F32 = jnp.float32
BF16 = jnp.bfloat16
ROWS_BY_ROWS = (((1,), (1,)), ((), ()))


def layer_norm(values):
    mean = jnp.mean(values, axis=-1, keepdims=True)
    centred = values - mean
    var = jnp.mean(centred * centred, axis=-1, keepdims=True)
    return centred * lax.rsqrt(var + EPS)


def silu_of_twice(half):
    return half + half * jnp.tanh(half)


def dot_t(a, b, **kw):
    return lax.dot_general(a, b, ROWS_BY_ROWS, preferred_element_type=F32, **kw)


def kernel(
    lengths,
    history,
    ln_gain_hbm,
    w_proj,
    w_out,
    pool_query_hbm,
    slots_hbm,
    cand_ids_hbm,
    item_table,
    w_rank,
    b_rank_hbm,
    w_score_hbm,
    layer_out,
    scores,
    hist,
    ln_gain,
    pool_query,
    slots,
    cand_ids,
    b_rank,
    w_score,
    wp,
    wo,
    table,
    wr,
    normed,
    gate,
    qkv,
    kv,
    qs,
    acc,
    back,
    att,
    masks,
    cand,
    pre,
    part,
    parts,
    told,
    pieces,
    chosen,
    interests,
    vectors,
    share,
    shares,
    load_sem,
    kv_send,
    kv_recv,
    q_send,
    q_recv,
    pass_send,
    pass_recv,
    back_send,
    back_recv,
    sum_sem,
    state_sem,
    pick_sem,
    over_send,
    chain_send,
    chain_recv,
    spread_sem,
    twin_sem,
):
    events, width = hist.shape
    head_size = width // HEADS
    plane, line, ranks = parts.shape[0], pieces.shape[0], wr.shape[0]
    t = lax.axis_index("tm")
    owner = lax.axis_index("users")
    mp = lax.axis_index("mp")
    user = owner * ranks + mp
    x, y = lax.div(t, SIDE), lax.rem(t, SIDE)
    core = lax.rem(mp, 2)

    def even(v):
        return v + 1 - 2 * lax.rem(v, 2)

    def odd(v):
        return SIDE - 1 - v

    def swap_y(v):
        return even(v) + core * (odd(v) - even(v))

    def ring_y(v):
        return odd(v) + core * (even(v) - odd(v))

    def head_of(a, b):
        first = lax.rem(lax.div(b + 1, 2), 2)
        return 2 * lax.div(a, 2) + first + core * (lax.div(b, 2) - first)

    def moved(a, b, rel):
        first, second = lax.rem(rel, 2), lax.div(rel, 2)
        return a + second * (odd(a) - a), b + first * (swap_y(b) - b)

    def in_plane(a, b):
        return {"tm": a * SIDE + b}

    head = head_of(x, y)

    depth = wr.shape[1] // SIDE
    last = line // ranks - 1
    twin = mp + 1 - 2 * core
    across = lax.rem(mp + 2, ranks)
    near = jnp.minimum(owner, last - owner)
    step_on = jnp.where(owner < near + 1, 1, -1)
    ends_at = last // 2

    def weights_of(whose):
        return wr.at[whose, pl.ds(pl.multiple_of(y * depth, depth), depth)]

    def chain_copies(whose, to, sems):
        return [
            pltpu.make_async_remote_copy(
                src_ref=ref,
                dst_ref=ref,
                send_sem=sems.at[n],
                recv_sem=chain_recv.at[n],
                device_id=to,
                device_id_type=MESH,
            )
            for n, ref in enumerate((weights_of(whose), vectors.at[whose]))
        ]

    over = {"users": last - owner, "mp": across}
    onward = {"users": owner + step_on}

    def relay(j):
        @pl.when(near == j)
        def _():
            for copy in chain_copies(across, onward, chain_send):
                copy.wait_recv()
                if j < ends_at:
                    copy.start()

    loads = [pltpu.make_async_copy(history.at[0], hist, load_sem.at[0])]
    for n, block in enumerate((3, 1, 2, 0)):
        cols = pl.ds(block * width, width)
        loads.append(pltpu.make_async_copy(w_proj.at[:, cols], wp.at[n], load_sem.at[n + 1]))
    rest = (
        (ln_gain_hbm, ln_gain),
        (pool_query_hbm, pool_query),
        (slots_hbm, slots),
        (cand_ids_hbm, cand_ids),
        (b_rank_hbm, b_rank),
        (w_score_hbm, w_score),
        (w_out, wo),
        (item_table, table),
        (w_rank, wr.at[mp]),
    )
    for n, (src, dst) in enumerate(rest):
        loads.append(pltpu.make_async_copy(src, dst, load_sem.at[5 + n]))
    loads[0].start()
    loads[5].start()
    for load in loads[1:5] + loads[6:]:
        load.start()

    pieces[...] = jnp.zeros_like(pieces)

    barrier = pltpu.get_barrier_semaphore()
    height = line // 2
    low = height // 2
    level = lax.div(mp, 2) * low + owner

    levels = []
    for k in range(height - 1):
        chip = lax.rem(level + low + (k + 1) // 2 * (1 - 2 * (k % 2)), height)
        levels.append({"users": lax.rem(chip, low), "mp": 2 * lax.div(chip, low) + core})

    def along(a, b):
        return {"tm": lax.rem(x + a, SIDE) * SIDE + lax.rem(y + b, SIDE)}

    def along_y(b, other):
        return {"tm": x * SIDE + lax.rem(y + b, SIDE), "mp": mp + other * (1 - 2 * core)}

    greeted = [along(a, b) for a, b in STEPS] + [along_y(b, 1) for b in range(SIDE)]
    greeted = levels + greeted
    for device in greeted:
        pl.semaphore_signal(barrier, inc=1, device_id=device, device_id_type=MESH)

    first_pos = t * events
    length = lengths[0]
    pos = first_pos + lax.broadcasted_iota(jnp.int32, (events, 1), 0)
    live = pos < length
    loads[0].wait()
    loads[5].wait()
    normed[...] = (layer_norm(hist[...].astype(F32)) * ln_gain[...]).astype(BF16)

    def project(n):
        loads[n + 1].wait()
        half = 0.5 * jnp.dot(normed[...], wp[n], preferred_element_type=F32)
        return silu_of_twice(half)

    keys = project(0).astype(BF16)
    for h in range(HEADS):
        qkv[h, 0] = keys[:, h * head_size : (h + 1) * head_size]
    values = jnp.where(live, project(1), 0.0).astype(BF16)
    for h in range(HEADS):
        qkv[h, 1] = values[:, h * head_size : (h + 1) * head_size]

    pl.semaphore_wait(barrier, len(greeted))

    kv_copies, q_copies = [], []
    for rel in (3, 2, 1):
        a, b = moved(x, y, rel)
        for n in range(2):
            copy = pltpu.make_async_remote_copy(
                src_ref=qkv.at[head_of(a, b), n],
                dst_ref=kv.at[rel, n],
                send_sem=kv_send.at[rel, n],
                recv_sem=kv_recv.at[rel, n],
                device_id=in_plane(a, b),
                device_id_type=MESH,
            )
            copy.start()
            kv_copies.append(copy)

    query = (project(2) * (0.5 * head_size**-0.5)).astype(BF16)
    for h in range(HEADS):
        qkv[h, 2] = query[:, h * head_size : (h + 1) * head_size]
    for rel in (3, 2, 1):
        a, b = moved(x, y, rel)
        copy = pltpu.make_async_remote_copy(
            src_ref=qkv.at[head_of(a, b), 2],
            dst_ref=qs.at[rel],
            send_sem=q_send.at[rel],
            recv_sem=q_recv.at[rel],
            device_id=in_plane(a, b),
            device_id_type=MESH,
        )
        copy.start()
        q_copies.append(copy)
    for load in loads[9:11] + loads[13:]:
        load.wait()
    vectors[mp, 0:1] = b_rank[...]
    vectors[mp, 1:2] = w_score[...]

    @pl.when(near == 0)
    def _():
        for copy in chain_copies(mp, over, over_send):
            copy.start()

    kv[0] = qkv[head, pl.ds(0, 2)]
    qs[0] = qkv[head, 2]

    x_near, y_near = even(x), ring_y(y)

    def pass_kv(n, m):
        return pltpu.make_async_remote_copy(
            src_ref=kv.at[n, m],
            dst_ref=kv.at[HEADS + n, m],
            send_sem=pass_send.at[m, n],
            recv_sem=pass_recv.at[m, n],
            device_id=in_plane(x_near, y),
            device_id_type=MESH,
        )

    def pass_q(n):
        return pltpu.make_async_remote_copy(
            src_ref=qs.at[n],
            dst_ref=qs.at[HEADS + n],
            send_sem=pass_send.at[2, n],
            recv_sem=pass_recv.at[2, n],
            device_id=in_plane(x, y_near),
            device_id_type=MESH,
        )

    def back_copy(n, which):
        a, b = moved(x, y_near if which else y, n)
        return pltpu.make_async_remote_copy(
            src_ref=back.at[which, n],
            dst_ref=att.at[which, head],
            send_sem=back_send.at[which, n],
            recv_sem=back_recv.at[which, n],
            device_id=in_plane(a, b),
            device_id_type=MESH,
        )

    pass_q(0).start()
    for m in range(2):
        pass_kv(0, m).start()

    gate[...] = project(3).astype(BF16)
    acc[...] = jnp.zeros_like(acc)

    owned, count = cand_ids.shape
    pool = table.shape[0]
    for load in loads[6:9] + loads[11:13]:
        load.wait()

    @pl.loop(0, owned)
    def _(r):
        @pl.when(r > 0)
        def _():
            for m in range(2):
                pltpu.make_async_copy(kv.at[r, m], kv.at[r, m], kv_recv.at[r, m]).wait()
                pass_kv(r, m).start()

        eye = lax.broadcasted_iota(jnp.int32, (count, count), 0) == lax.broadcasted_iota(
            jnp.int32, (count, count), 1
        )
        item = lax.broadcasted_iota(jnp.int32, (count, pool), 1).astype(F32)
        ids = cand_ids[pl.ds(r, 1), :].astype(F32)
        column = jnp.sum(jnp.where(eye, ids, 0.0), axis=1, keepdims=True)
        onehot = jnp.where(item == column, 1.0, 0.0).astype(BF16)
        cand[pl.ds(r * count, count)] = jnp.dot(
            onehot, table[...], preferred_element_type=F32
        ).astype(BF16)

    pairs = 2 * events
    behind = lax.broadcasted_iota(jnp.int32, (events, events), 0) >= lax.broadcasted_iota(
        jnp.int32, (events, events), 1
    )
    masks[0] = jnp.zeros((events, events), F32)
    masks[1] = jnp.where(behind, 1.0, 0.0)
    masks[2] = jnp.ones((events, events), F32)

    def rows_of(which, pair):
        return pl.ds(pl.multiple_of((2 * which + pair) * pairs, pairs), pairs)

    def attend(q_set, q_pair, k_set, k_pair, masked):
        q_first, k_first = HEADS * q_set + 2 * q_pair, HEADS * k_set + 2 * k_pair
        query = qs[pl.ds(q_first, 2)].reshape(pairs, head_size)
        half = jnp.concatenate(
            [dot_t(query, kv[k_first + n, 0]) for n in range(2)], axis=1
        )
        if masked:
            q_y = y_near if q_set else y
            half = jnp.concatenate(
                [
                    jnp.concatenate(
                        [
                            half[a * events : (a + 1) * events, b * events : (b + 1) * events]
                            * masks[1 + jnp.clip(q_row - k_row, -1, 1)]
                            for b, k_row in enumerate((y, swap_y(y)))
                        ],
                        axis=1,
                    )
                    for a, q_row in enumerate((q_y, swap_y(q_y)))
                ],
                axis=0,
            )
        weights = silu_of_twice(half).astype(BF16)
        value = jnp.concatenate([kv[k_first + n, 1] for n in range(2)], axis=0)
        acc[rows_of(q_set, q_pair)] += jnp.dot(weights, value, preferred_element_type=F32)

    late = jnp.where(x < SIDE // 2, 1, 0)
    early = 1 - late
    outer = jnp.logical_or(x == 0, x == SIDE - 1)

    def attend_own(q_set):
        for pair in range(2):
            attend(q_set, pair, 0, pair, True)
        attend(q_set, late, 0, early, False)

    def attend_near(q_set, n):
        q_pair = late if n else jnp.where(outer, late, early)
        k_pair = jnp.where(outer, n, jnp.where(x == 1, 0, 1))
        attend(q_set, q_pair, 1, k_pair, False)

    for n in range(1, HEADS):
        pltpu.make_async_copy(qs.at[n], qs.at[n], q_recv.at[n]).wait()
        pass_q(n).start()
    attend_own(0)
    relay(0)
    for n in range(HEADS):
        pass_q(n).wait_recv()
    attend(1, 0, 0, 0, True)
    attend(1, 1, 0, 1, True)
    attend(1, late, 0, early, False)
    for n in range(HEADS):
        for m in range(2):
            pass_kv(n, m).wait_recv()
    def send_back(which, pair):
        for m in (1, 0):
            n = 2 * pair + m
            rows = pl.ds(pl.multiple_of((HEADS * which + n) * events, events), events)
            summed = acc[rows].astype(BF16)
            away = n >= 1 - which

            @pl.when(away)
            def _():
                back[which, n] = summed
                back_copy(n, which).start()

            @pl.when(jnp.logical_not(away))
            def _():
                att[which, head] = summed

    attend_near(1, 0)
    send_back(1, early)
    attend_near(1, 1)
    send_back(1, late)
    relay(1)
    attend_near(0, 0)
    send_back(0, early)
    attend_near(0, 1)
    send_back(0, late)
    relay(2)
    for n in range(HEADS):
        back_copy(n, 1).wait_recv()
    for n in range(1, HEADS):
        back_copy(n, 0).wait_recv()

    own_half = lax.div(mp, 2)
    attended = jnp.concatenate(
        [att[0, h].astype(F32) + att[1, h].astype(F32) for h in range(HEADS)], axis=1
    )
    mixed = (layer_norm(attended) * gate[...].astype(F32)).astype(BF16)
    projected = jnp.dot(mixed, wo[...], preferred_element_type=F32)
    out = (hist[...].astype(F32) + projected).astype(BF16)
    layer_out[0] = out
    groups = pool_query.shape[0]
    half = 0.5 * dot_t(pool_query[...], out)
    lane = first_pos + lax.broadcasted_iota(jnp.int32, half.shape, 1)
    pool_w = jnp.where(lane < length, silu_of_twice(half), 0.0).astype(BF16)
    sums = jnp.dot(pool_w, out, preferred_element_type=F32)

    for g in range(groups):
        part[g] = sums[g : g + 1]
    for a, b in STEPS:
        pltpu.make_async_remote_copy(
            src_ref=part.at[lax.rem(y + b, SIDE)],
            dst_ref=parts.at[t],
            send_sem=sum_sem.at[0],
            recv_sem=sum_sem.at[1],
            device_id=along(a, b),
            device_id_type=MESH,
        ).start()

    def wait_for(buffer, many, sem):
        some = buffer.at[pl.ds(0, many)]
        pltpu.make_async_copy(some, some, sem).wait()

    parts[t] = part[y]
    relay(3)
    quarter = weights_of(across)
    for b in (2, 1, 3):
        pltpu.make_async_remote_copy(
            src_ref=quarter,
            dst_ref=quarter,
            send_sem=spread_sem.at[0],
            recv_sem=spread_sem.at[1],
            device_id=along(0, b),
            device_id_type=MESH,
        ).start()
    others = wr.at[across, pl.ds(0, (SIDE - 1) * depth)]
    pre[own_half] = jnp.dot(cand[...], wr[mp, :width], preferred_element_type=F32)
    wait_for(parts, plane - 1, sum_sem.at[1])
    state = jnp.sum(parts[...], axis=0).astype(BF16).astype(F32)

    own_interest = layer_norm(state).astype(BF16).astype(F32)
    told[...] = own_interest
    pieces[user] = own_interest

    for device in levels:
        pltpu.make_async_remote_copy(
            src_ref=told,
            dst_ref=pieces.at[user],
            send_sem=state_sem.at[0],
            recv_sem=state_sem.at[1],
            device_id=device,
            device_id_type=MESH,
        ).start()

    wait_for(pieces, height - 1, state_sem.at[1])
    mine = owner * owned + lax.broadcasted_iota(jnp.int32, (owned, line), 0)
    picker = jnp.where(slots[...] == mine, 1.0, 0.0).astype(BF16)
    known = pieces[...].reshape(line, width).astype(BF16)
    own_slots = jnp.dot(picker, known, preferred_element_type=F32)
    chosen[...] = own_slots
    interests[core * SIDE + y] = own_slots
    for b, n in ((2, 0), (2, 1), (1, 0), (3, 0), (1, 1), (3, 1), (0, 1)):
        pltpu.make_async_remote_copy(
            src_ref=chosen,
            dst_ref=interests.at[core * SIDE + y],
            send_sem=pick_sem.at[0],
            recv_sem=pick_sem.at[1],
            device_id=along_y(b, n),
            device_id_type=MESH,
        ).start()

    pltpu.make_async_copy(others, others, spread_sem.at[1]).wait()
    pre[1 - own_half] = jnp.dot(cand[...], wr[across, :width], preferred_element_type=F32)
    wait_for(interests, 2 * SIDE - 1, pick_sem.at[1])

    interest = jnp.concatenate(
        [interests[g] + interests[SIDE + g] for g in range(groups)], axis=0
    ).astype(BF16)
    half = (0.5 * width**-0.5) * dot_t(cand[...], interest)
    row = lax.div(lax.broadcasted_iota(jnp.int32, half.shape, 0), count)
    column = lax.rem(lax.broadcasted_iota(jnp.int32, half.shape, 1), owned)
    attn = jnp.where(row == column, silu_of_twice(half), 0.0)
    high = attn.astype(BF16)
    low = (attn - high.astype(F32)).astype(BF16)
    factors = jnp.concatenate([high, low, high], axis=1)
    terms = jnp.zeros_like(pre[0])
    for n in range(2):
        block = core + 2 * n
        mixed_in = jnp.dot(interest, wr[block, width:], preferred_element_type=F32)
        large = mixed_in.astype(BF16)
        small = (mixed_in - large.astype(F32)).astype(BF16)
        more = jnp.dot(
            factors, jnp.concatenate([large, large, small], axis=0), preferred_element_type=F32
        )
        half = 0.5 * (pre[n] + vectors[block, 0:1] + more)
        terms += silu_of_twice(half) * vectors[block, 1:2]
    high = terms.astype(BF16)
    low = (terms - high.astype(F32)).astype(BF16)
    ones = jnp.ones((16, terms.shape[1]), BF16)
    own_share = (dot_t(ones, high) + dot_t(ones, low))[0:1]
    share[...] = own_share
    shares[core] = own_share
    exchange = pltpu.make_async_remote_copy(
        src_ref=share,
        dst_ref=shares.at[core],
        send_sem=twin_sem.at[0],
        recv_sem=twin_sem.at[1],
        device_id={"mp": twin},
        device_id_type=MESH,
    )
    exchange.start()
    exchange.wait_recv()
    total = jnp.sum(shares[...], axis=0)
    for r in range(owned):
        scores[r : r + 1, :] = total[0:1, r * count : (r + 1) * count]

    for copy in kv_copies + q_copies:
        copy.wait_send()
    for n in range(HEADS):
        for m in range(2):
            pass_kv(n, m).wait_send()
        pass_q(n).wait_send()
        back_copy(n, 1).wait_send()
    for n in range(1, HEADS):
        back_copy(n, 0).wait_send()
    wait_for(parts, plane - 1, sum_sem.at[0])
    wait_for(pieces, height - 1, state_sem.at[0])
    wait_for(interests, 2 * SIDE - 1, pick_sem.at[0])
    exchange.wait_send()

    pltpu.make_async_copy(others, others, spread_sem.at[0]).wait()

    @pl.when(near == 0)
    def _():
        for copy in chain_copies(mp, over, over_send):
            copy.wait_send()

    @pl.when(near < ends_at)
    def _():
        for copy in chain_copies(across, onward, chain_send):
            copy.wait_send()


def solution(mesh):
    plane, owners, ranks = mesh.shape["tm"], mesh.shape["users"], mesh.shape["mp"]
    line = owners * ranks

    def shards(
        history,
        ln_gain,
        w_proj,
        w_out,
        pool_query,
        lengths,
        slots,
        cand_ids,
        item_table,
        w_rank,
        b_rank,
        w_score,
    ):
        _, events, width = history.shape
        head_size = width // HEADS
        groups = pool_query.shape[0]
        owned, count = cand_ids.shape
        cands = owned * count
        hidden = w_rank.shape[1]
        vmem = pl.BlockSpec(memory_space=pltpu.VMEM)
        smem = pl.BlockSpec(memory_space=pltpu.SMEM)
        hbm = pl.BlockSpec(memory_space=pltpu.HBM)
        dma = pltpu.SemaphoreType.DMA
        return pl.pallas_call(
            kernel,
            out_shape=(
                jax.ShapeDtypeStruct(history.shape, BF16),
                jax.ShapeDtypeStruct((owned, count), F32),
            ),
            in_specs=[smem] + [hbm] * 11,
            out_specs=(vmem, vmem),
            scratch_shapes=[
                pltpu.VMEM((events, width), BF16),
                pltpu.VMEM((1, width), F32),
                pltpu.VMEM(pool_query.shape, BF16),
                pltpu.VMEM((1, line), jnp.int32),
                pltpu.VMEM((owned, count), jnp.int32),
                pltpu.VMEM((1, hidden), F32),
                pltpu.VMEM((1, hidden), F32),
                pltpu.VMEM((4, width, width), BF16),
                pltpu.VMEM((width, width), BF16),
                pltpu.VMEM(item_table.shape, BF16),
                pltpu.VMEM((ranks, *w_rank.shape), BF16),
                pltpu.VMEM((events, width), BF16),
                pltpu.VMEM((events, width), BF16),
                pltpu.VMEM((HEADS, 3, events, head_size), BF16),
                pltpu.VMEM((2 * HEADS, 2, events, head_size), BF16),
                pltpu.VMEM((2 * HEADS, events, head_size), BF16),
                pltpu.VMEM((2 * HEADS * events, head_size), F32),
                pltpu.VMEM((2, HEADS, events, head_size), BF16),
                pltpu.VMEM((2, HEADS, events, head_size), BF16),
                pltpu.VMEM((3, events, events), F32),
                pltpu.VMEM((cands, width), BF16),
                pltpu.VMEM((2, cands, hidden), F32),
                pltpu.VMEM((groups, 1, width), F32),
                pltpu.VMEM((plane, 1, width), F32),
                pltpu.VMEM((1, width), F32),
                pltpu.VMEM((line, 1, width), F32),
                pltpu.VMEM((owned, width), F32),
                pltpu.VMEM((2 * SIDE, owned, width), F32),
                pltpu.VMEM((ranks, 2, hidden), F32),
                pltpu.VMEM((1, cands), F32),
                pltpu.VMEM((2, 1, cands), F32),
                dma((14,)),
                dma((HEADS, 2)),
                dma((HEADS, 2)),
                dma((HEADS,)),
                dma((HEADS,)),
                dma((3, HEADS)),
                dma((3, HEADS)),
                dma((2, HEADS)),
                dma((2, HEADS)),
                dma((2,)),
                dma((2,)),
                dma((2,)),
                dma((2,)),
                dma((2,)),
                dma((2,)),
                dma((2,)),
                dma((2,)),
            ],
            compiler_params=pltpu.CompilerParams(
                collective_id=0, has_side_effects=True, vmem_limit_bytes=VMEM_BYTES
            ),
            cost_estimate=pl.CostEstimate(
                flops=4_000_000_000, bytes_accessed=6_000_000, transcendentals=5_000_000
            ),
        )(
            lengths,
            history,
            ln_gain.reshape(1, -1),
            w_proj,
            w_out,
            pool_query,
            slots.reshape(1, -1),
            cand_ids,
            item_table,
            w_rank,
            b_rank.reshape(1, -1),
            w_score.reshape(1, -1),
        )

    placed = (
        P(("users", "mp"), "tm", None),
        P(),
        P(),
        P(),
        P(),
        P(("users", "mp")),
        P(),
        P("users", "tm"),
        P("users", None),
        P(None, "mp"),
        P("mp"),
        P("mp"),
    )
    return jax.shard_map(
        shards,
        mesh=mesh,
        in_specs=placed,
        out_specs=(P(("users", "mp"), "tm", None), P("users", "tm")),
        check_vma=False,
    )
```

profile of v0, /device:TPU:1, one launch (start us, length us, event | category | flops | bytes accessed | tf_op | source)
XLA Modules:
  0.0 63.6 jit_solution(15569675956117505977)
XLA Ops:
  1.3 59.4 %shard_map.131 = (bf16[1,256,512]{2,1,0:T(8,128)(2,1)}, f32[4,64]{1,0:T(4,128)}) custom-call(s32[1]{0:T(128)S(6)} %copy.16.lengths, bf16[1,256,512]{2,1,0:T(8,128)(2,1)} %history.1, f32[1,512]{1,0:T(1,128)} %bitcast.4, bf16[512,2048]{1,0:T(8,128)(2,1)} %w_proj.1, bf16[512,512]{1,0:T(8,128)(2,1)} %w_out.1, bf16[4,512]{1,0:T(4,128)(2,1)} %pool_query_hbm.1, ...), custom_call_target="tpu_custom_call" | custom-call | flops 4000000000 | bytes 6000000 | tf_op jit(solution)/shard_map/pallas_call | solution.py:618
  60.6 1.7 %copy.17 = bf16[1,256,512]{2,1,0:T(8,128)(2,1)} copy(bf16[1,256,512]{2,1,0:T(8,128)(2,1)} %get-tuple-element.4) | data formatting | bytes 524288
  62.3 1.2 %copy.18 = f32[4,64]{1,0:T(4,128)} copy(f32[4,64]{1,0:T(4,128)} %get-tuple-element.5) | data formatting | bytes 2048
where the time goes:
time: 63.7 us; the launch traced here: 63.6 us
  Pallas kernels  59.4 us (93%)
  local copies, waits for them, and re-layouts  2.92 us (5%)
  between operations  1.29 us (2%)
    pallas_call x1, Pallas kernels, shards(): pl.pallas_call(kernel, out_shape=(jax.ShapeDtypeStruct(history.shape, BF1...  59.4 us
    unnamed x2, local copies, waits for them, and re-layouts  2.92 us

commit v1 on v0

--- a/solution.py
+++ b/solution.py
@@ -315,32 +315,12 @@
     for m in range(2):
         pass_kv(0, m).start()
 
-    gate[...] = project(3).astype(BF16)
     acc[...] = jnp.zeros_like(acc)
 
-    owned, count = cand_ids.shape
-    pool = table.shape[0]
-    for load in loads[6:9] + loads[11:13]:
-        load.wait()
-
-    @pl.loop(0, owned)
-    def _(r):
-        @pl.when(r > 0)
-        def _():
-            for m in range(2):
-                pltpu.make_async_copy(kv.at[r, m], kv.at[r, m], kv_recv.at[r, m]).wait()
-                pass_kv(r, m).start()
-
-        eye = lax.broadcasted_iota(jnp.int32, (count, count), 0) == lax.broadcasted_iota(
-            jnp.int32, (count, count), 1
-        )
-        item = lax.broadcasted_iota(jnp.int32, (count, pool), 1).astype(F32)
-        ids = cand_ids[pl.ds(r, 1), :].astype(F32)
-        column = jnp.sum(jnp.where(eye, ids, 0.0), axis=1, keepdims=True)
-        onehot = jnp.where(item == column, 1.0, 0.0).astype(BF16)
-        cand[pl.ds(r * count, count)] = jnp.dot(
-            onehot, table[...], preferred_element_type=F32
-        ).astype(BF16)
+    for r in range(1, HEADS):
+        for m in range(2):
+            pltpu.make_async_copy(kv.at[r, m], kv.at[r, m], kv_recv.at[r, m]).wait()
+            pass_kv(r, m).start()
 
     pairs = 2 * events
     behind = lax.broadcasted_iota(jnp.int32, (events, events), 0) >= lax.broadcasted_iota(
@@ -432,6 +412,26 @@
     attend_near(0, 1)
     send_back(0, late)
     relay(2)
+    gate[...] = project(3).astype(BF16)
+
+    owned, count = cand_ids.shape
+    pool = table.shape[0]
+    for load in loads[6:9] + loads[11:13]:
+        load.wait()
+
+    @pl.loop(0, owned)
+    def _(r):
+        eye = lax.broadcasted_iota(jnp.int32, (count, count), 0) == lax.broadcasted_iota(
+            jnp.int32, (count, count), 1
+        )
+        item = lax.broadcasted_iota(jnp.int32, (count, pool), 1).astype(F32)
+        ids = cand_ids[pl.ds(r, 1), :].astype(F32)
+        column = jnp.sum(jnp.where(eye, ids, 0.0), axis=1, keepdims=True)
+        onehot = jnp.where(item == column, 1.0, 0.0).astype(BF16)
+        cand[pl.ds(r * count, count)] = jnp.dot(
+            onehot, table[...], preferred_element_type=F32
+        ).astype(BF16)
+
     for n in range(HEADS):
         back_copy(n, 1).wait_recv()
     for n in range(1, HEADS):

time: 63.7 us -> 63.7 us (level)
  no operation moved by 1% of the time
where the time goes in v1:
time: 63.7 us; the launch traced here: 63.6 us
  Pallas kernels  59.4 us (93%)
  local copies, waits for them, and re-layouts  2.92 us (5%)
  between operations  1.29 us (2%)
    pallas_call x1, Pallas kernels, shards(): pl.pallas_call(kernel, out_shape=(jax.ShapeDtypeStruct(history.shape, BF1...  59.4 us
    unnamed x2, local copies, waits for them, and re-layouts  2.92 us

profile of v1, /device:TPU:1, one launch (start us, length us, event | category | flops | bytes accessed | tf_op | source)
XLA Modules:
  0.0 63.6 jit_solution(10143247409332329325)
XLA Ops:
  1.3 59.4 %shard_map.131 = (bf16[1,256,512]{2,1,0:T(8,128)(2,1)}, f32[4,64]{1,0:T(4,128)}) custom-call(s32[1]{0:T(128)S(6)} %copy.16.lengths, bf16[1,256,512]{2,1,0:T(8,128)(2,1)} %history.1, f32[1,512]{1,0:T(1,128)} %bitcast.4, bf16[512,2048]{1,0:T(8,128)(2,1)} %w_proj.1, bf16[512,512]{1,0:T(8,128)(2,1)} %w_out.1, bf16[4,512]{1,0:T(4,128)(2,1)} %pool_query_hbm.1, ...), custom_call_target="tpu_custom_call" | custom-call | flops 4000000000 | bytes 6000000 | tf_op jit(solution)/shard_map/pallas_call | solution.py:618
  60.6 1.7 %copy.17 = bf16[1,256,512]{2,1,0:T(8,128)(2,1)} copy(bf16[1,256,512]{2,1,0:T(8,128)(2,1)} %get-tuple-element.4) | data formatting | bytes 524288
  62.3 1.2 %copy.18 = f32[4,64]{1,0:T(4,128)} copy(f32[4,64]{1,0:T(4,128)} %get-tuple-element.5) | data formatting | bytes 2048

commit v2 on v0

--- a/solution.py
+++ b/solution.py
@@ -209,7 +209,7 @@
         return {"tm": x * SIDE + lax.rem(y + b, SIDE), "mp": mp + other * (1 - 2 * core)}
 
     greeted = [along(a, b) for a, b in STEPS] + [along_y(b, 1) for b in range(SIDE)]
-    greeted = levels + greeted
+    greeted += levels
     for device in greeted:
         pl.semaphore_signal(barrier, inc=1, device_id=device, device_id_type=MESH)
 

time: 63.7 us -> 63.8 us (level)
  no operation moved by 1% of the time
where the time goes in v2:
time: 63.8 us; the launch traced here: 63.7 us
  Pallas kernels  59.5 us (93%)
  local copies, waits for them, and re-layouts  2.92 us (5%)
  between operations  1.29 us (2%)
    pallas_call x1, Pallas kernels, shards(): pl.pallas_call(kernel, out_shape=(jax.ShapeDtypeStruct(history.shape, BF1...  59.5 us
    unnamed x2, local copies, waits for them, and re-layouts  2.92 us

profile of v2, /device:TPU:1, one launch (start us, length us, event | category | flops | bytes accessed | tf_op | source)
XLA Modules:
  0.0 63.7 jit_solution(12397050903284958858)
XLA Ops:
  1.3 59.5 %shard_map.131 = (bf16[1,256,512]{2,1,0:T(8,128)(2,1)}, f32[4,64]{1,0:T(4,128)}) custom-call(s32[1]{0:T(128)S(6)} %copy.16.lengths, bf16[1,256,512]{2,1,0:T(8,128)(2,1)} %history.1, f32[1,512]{1,0:T(1,128)} %bitcast.4, bf16[512,2048]{1,0:T(8,128)(2,1)} %w_proj.1, bf16[512,512]{1,0:T(8,128)(2,1)} %w_out.1, bf16[4,512]{1,0:T(4,128)(2,1)} %pool_query_hbm.1, ...), custom_call_target="tpu_custom_call" | custom-call | flops 4000000000 | bytes 6000000 | tf_op jit(solution)/shard_map/pallas_call | solution.py:618
  60.7 1.7 %copy.17 = bf16[1,256,512]{2,1,0:T(8,128)(2,1)} copy(bf16[1,256,512]{2,1,0:T(8,128)(2,1)} %get-tuple-element.4) | data formatting | bytes 524288
  62.4 1.2 %copy.18 = f32[4,64]{1,0:T(4,128)} copy(f32[4,64]{1,0:T(4,128)} %get-tuple-element.5) | data formatting | bytes 2048

commit v3 on v0

--- a/solution.py
+++ b/solution.py
@@ -468,6 +468,25 @@
         pltpu.make_async_copy(some, some, sem).wait()
 
     parts[t] = part[y]
+    others = wr.at[across, pl.ds(0, (SIDE - 1) * depth)]
+    pre[own_half] = jnp.dot(cand[...], wr[mp, :width], preferred_element_type=F32)
+    wait_for(parts, plane - 1, sum_sem.at[1])
+    state = jnp.sum(parts[...], axis=0).astype(BF16).astype(F32)
+
+    own_interest = layer_norm(state).astype(BF16).astype(F32)
+    told[...] = own_interest
+    pieces[user] = own_interest
+
+    for device in levels:
+        pltpu.make_async_remote_copy(
+            src_ref=told,
+            dst_ref=pieces.at[user],
+            send_sem=state_sem.at[0],
+            recv_sem=state_sem.at[1],
+            device_id=device,
+            device_id_type=MESH,
+        ).start()
+
     relay(3)
     quarter = weights_of(across)
     for b in (2, 1, 3):
@@ -479,25 +498,6 @@
             device_id=along(0, b),
             device_id_type=MESH,
         ).start()
-    others = wr.at[across, pl.ds(0, (SIDE - 1) * depth)]
-    pre[own_half] = jnp.dot(cand[...], wr[mp, :width], preferred_element_type=F32)
-    wait_for(parts, plane - 1, sum_sem.at[1])
-    state = jnp.sum(parts[...], axis=0).astype(BF16).astype(F32)
-
-    own_interest = layer_norm(state).astype(BF16).astype(F32)
-    told[...] = own_interest
-    pieces[user] = own_interest
-
-    for device in levels:
-        pltpu.make_async_remote_copy(
-            src_ref=told,
-            dst_ref=pieces.at[user],
-            send_sem=state_sem.at[0],
-            recv_sem=state_sem.at[1],
-            device_id=device,
-            device_id_type=MESH,
-        ).start()
-
     wait_for(pieces, height - 1, state_sem.at[1])
     mine = owner * owned + lax.broadcasted_iota(jnp.int32, (owned, line), 0)
     picker = jnp.where(slots[...] == mine, 1.0, 0.0).astype(BF16)

time: 63.7 us -> 63.6 us (level)
  no operation moved by 1% of the time
where the time goes in v3:
time: 63.6 us; the launch traced here: 63.4 us
  Pallas kernels  59.2 us (93%)
  local copies, waits for them, and re-layouts  2.92 us (5%)
  between operations  1.29 us (2%)
    pallas_call x1, Pallas kernels, shards(): pl.pallas_call(kernel, out_shape=(jax.ShapeDtypeStruct(history.shape, BF1...  59.2 us
    unnamed x2, local copies, waits for them, and re-layouts  2.92 us

profile of v3, /device:TPU:1, one launch (start us, length us, event | category | flops | bytes accessed | tf_op | source)
XLA Modules:
  0.0 63.4 jit_solution(5244577088440059343)
XLA Ops:
  1.3 59.2 %shard_map.131 = (bf16[1,256,512]{2,1,0:T(8,128)(2,1)}, f32[4,64]{1,0:T(4,128)}) custom-call(s32[1]{0:T(128)S(6)} %copy.16.lengths, bf16[1,256,512]{2,1,0:T(8,128)(2,1)} %history.1, f32[1,512]{1,0:T(1,128)} %bitcast.4, bf16[512,2048]{1,0:T(8,128)(2,1)} %w_proj.1, bf16[512,512]{1,0:T(8,128)(2,1)} %w_out.1, bf16[4,512]{1,0:T(4,128)(2,1)} %pool_query_hbm.1, ...), custom_call_target="tpu_custom_call" | custom-call | flops 4000000000 | bytes 6000000 | tf_op jit(solution)/shard_map/pallas_call | solution.py:618
  60.5 1.7 %copy.17 = bf16[1,256,512]{2,1,0:T(8,128)(2,1)} copy(bf16[1,256,512]{2,1,0:T(8,128)(2,1)} %get-tuple-element.4) | data formatting | bytes 524288
  62.1 1.2 %copy.18 = f32[4,64]{1,0:T(4,128)} copy(f32[4,64]{1,0:T(4,128)} %get-tuple-element.5) | data formatting | bytes 2048
